TPU v7x, 256 devices: a whole 4x4x8 slice. The times are simulated.
256 devices in a mesh: batch: 4 (over y), expert: 64 (over x, z, core).
Axes of the slice: x: 4, y: 4, z: 8, core: 2. Of those that a mesh axis runs over, the one named last changes fastest.
Arguments:
- tokens: bfloat16 [32768, 1024], P(('batch', 'expert')), may hold values from -6 to 6
- cotangent: bfloat16 [32768, 1024], P(('batch', 'expert')), may hold values from -6 to 6
- domain_ids: int32 [32768], P(('batch', 'expert')), may hold values from 0 to 7
- shared_ids: int32 [32768, 2], P(('batch', 'expert')), may hold values from 0 to 63, all different within a row
- private_ids: int32 [32768, 2], P(('batch', 'expert')), may hold values from 0 to 7, all different within a row
- gate_weight: bfloat16 [1024, 8, 72], replicated, may hold values from -0.375 to 0.375
- shared_in: bfloat16 [64, 1024, 2048], P('expert', None, 'batch'), may hold values from -0.1875 to 0.1875
- shared_out: bfloat16 [64, 2048, 1024], P('expert', 'batch'), may hold values from -0.125 to 0.125
- private_in: bfloat16 [64, 1024, 2048], P('expert', None, 'batch'), may hold values from -0.1875 to 0.1875
- private_out: bfloat16 [64, 2048, 1024], P('expert', 'batch'), may hold values from -0.125 to 0.125
Outputs:
- mixed: bfloat16 [32768, 1024], P(('batch', 'expert'))
- grad_shared_in: bfloat16 [64, 1024, 2048], P('expert', None, 'batch')
- grad_shared_out: bfloat16 [64, 2048, 1024], P('expert', 'batch')
- grad_private_in: bfloat16 [64, 1024, 2048], P('expert', None, 'batch')
- grad_private_out: bfloat16 [64, 2048, 1024], P('expert', 'batch')
- grad_gate: float32 [1024, 8, 72], P(('batch', 'expert'))
All inputs are finite; a program needn't handle non-finite values.
Results may differ from a plain program's by a relative error of at most 0.015.
Values may be sent and summed in bfloat16 or wider, within the bound.
No kernel may reach another device: no remote copies, remote signals or barrier semaphores. Data moves between devices by JAX's collectives and lax.ppermute only.
A program may use at most 128 MiB of HBM per device.

v0:
```python
import jax
import jax.numpy as jnp
from jax import lax
from jax.sharding import PartitionSpec as P

SHARED = 64
PRIV = 8
DOMAINS = 8
PRIVATE = 64
GATES = 72
CAP = 4


def silu_slope(values):
    sigmoid = jax.nn.sigmoid(values)
    return sigmoid * (1.0 + values * (1.0 - sigmoid))


def routing(expert_ids, number, height):
    experts = jnp.arange(number, dtype=jnp.int32)
    onehot = (expert_ids[:, :, None] == experts[None, None, :]).astype(jnp.float32)
    per_row = jnp.sum(onehot, axis=1)
    order = jnp.arange(height, dtype=jnp.int32)
    lower = (order[:, None] > order[None, :]).astype(jnp.bfloat16)
    earlier = jnp.dot(lower, per_row.astype(jnp.bfloat16), preferred_element_type=jnp.float32)
    slots = jnp.sum(onehot * earlier[:, None, :], axis=2).astype(jnp.int32)
    target = jnp.where(slots < CAP, expert_ids * CAP + slots, -1)
    cells = jnp.arange(number * CAP, dtype=jnp.int32)
    return [
        (cells[:, None] == target[None, :, pick_index]).astype(jnp.float32)
        for pick_index in range(2)
    ]


def pack_rows(selectors, tokens, features):
    placed = (selectors[0] + selectors[1]).astype(jnp.bfloat16)
    packed = jnp.dot(placed, tokens, preferred_element_type=jnp.float32)
    return packed.astype(jnp.bfloat16).reshape(-1, CAP, features)


def pack_scaled(selectors, gate_pair, cot_float, features):
    weighted = selectors[0] * gate_pair[None, :, 0] + selectors[1] * gate_pair[None, :, 1]
    packed = jnp.dot(weighted, cot_float, precision=lax.Precision.HIGHEST)
    return packed.astype(jnp.bfloat16).reshape(-1, CAP, features)


def unpack_rows(selector, returned, features):
    flat = returned.reshape(-1, features)
    return jnp.dot(selector.T.astype(jnp.bfloat16), flat, preferred_element_type=jnp.float32)


def forward_experts(inputs_x, weight_a, weight_b):
    pre = jnp.einsum("erd,edh->erh", inputs_x, weight_a, preferred_element_type=jnp.float32)
    act = jax.nn.silu(pre).astype(jnp.bfloat16)
    outputs = jnp.einsum("erh,ehd->erd", act, weight_b, preferred_element_type=jnp.float32)
    return (pre, act, outputs)


def backward_experts(pre, scaled, weight_b):
    slope = jnp.einsum("erd,ehd->erh", scaled, weight_b, preferred_element_type=jnp.float32)
    return (slope * silu_slope(pre)).astype(jnp.bfloat16)


def body(
    tokens,
    cotangent,
    domain_ids,
    shared_ids,
    private_ids,
    gate_weight,
    shared_in,
    shared_out,
    private_in,
    private_out,
):
    height, features = tokens.shape
    columns_all = DOMAINS * GATES
    table = jnp.dot(
        tokens, gate_weight.reshape(features, columns_all), preferred_element_type=jnp.float32
    )
    base = domain_ids[:, None] * GATES
    columns = jnp.concatenate([base + shared_ids, base + SHARED + private_ids], axis=1)
    picked = (
        columns[:, :, None] == jnp.arange(columns_all, dtype=jnp.int32)[None, None, :]
    ).astype(jnp.float32)
    logits = jnp.sum(table[:, None, :] * picked, axis=2)
    gates = jax.nn.softmax(logits, axis=1)
    shared_sel = routing(shared_ids, SHARED, height)
    private_sel = routing(domain_ids[:, None] * PRIV + private_ids, PRIVATE, height)
    send_shared = pack_rows(shared_sel, tokens, features)
    send_private = pack_rows(private_sel, tokens, features)
    cot_float = cotangent.astype(jnp.float32)
    scaled_shared = pack_scaled(shared_sel, gates[:, 0:2], cot_float, features)
    scaled_private = pack_scaled(private_sel, gates[:, 2:4], cot_float, features)
    got_shared, got_private = (
        lax.all_to_all(send_shared, "expert", split_axis=0, concat_axis=1, tiled=True),
        lax.all_to_all(send_private, "expert", split_axis=0, concat_axis=1, tiled=True),
    )
    full_shared_in, full_shared_out, full_private_in, full_private_out = (
        lax.all_gather(shared_in, "batch", axis=2, tiled=True),
        lax.all_gather(shared_out, "batch", axis=1, tiled=True),
        lax.all_gather(private_in, "batch", axis=2, tiled=True),
        lax.all_gather(private_out, "batch", axis=1, tiled=True),
    )
    pre_shared, act_shared, out_shared = forward_experts(
        got_shared, full_shared_in, full_shared_out
    )
    pre_private, act_private, out_private = forward_experts(
        got_private, full_private_in, full_private_out
    )
    back_shared, back_private = (
        lax.all_to_all(
            out_shared.astype(jnp.bfloat16), "expert", split_axis=1, concat_axis=0, tiled=True
        ),
        lax.all_to_all(
            out_private.astype(jnp.bfloat16), "expert", split_axis=1, concat_axis=0, tiled=True
        ),
    )
    pick_outputs = [unpack_rows(selector, back_shared, features) for selector in shared_sel]
    pick_outputs = pick_outputs + [
        unpack_rows(selector, back_private, features) for selector in private_sel
    ]
    mixed = gates[:, 0:1] * pick_outputs[0] + gates[:, 1:2] * pick_outputs[1]
    mixed = mixed + gates[:, 2:3] * pick_outputs[2] + gates[:, 3:4] * pick_outputs[3]
    dgate = jnp.stack(
        [jnp.sum(cot_float * output_rows, axis=1) for output_rows in pick_outputs], axis=1
    )
    dlogit = gates * (dgate - jnp.sum(gates * dgate, axis=1, keepdims=True))
    spread = jnp.sum(dlogit[:, :, None] * picked, axis=1)
    gate_term = jnp.dot(
        tokens.astype(jnp.float32).T, spread, precision=lax.Precision.HIGHEST
    ).reshape(features, DOMAINS, GATES)
    grad_gate = lax.psum_scatter(gate_term, ("batch", "expert"), scatter_dimension=0, tiled=True)
    got_gshared, got_gprivate = (
        lax.all_to_all(scaled_shared, "expert", split_axis=0, concat_axis=1, tiled=True),
        lax.all_to_all(scaled_private, "expert", split_axis=0, concat_axis=1, tiled=True),
    )
    back_grad_shared = backward_experts(pre_shared, got_gshared, full_shared_out)
    back_grad_private = backward_experts(pre_private, got_gprivate, full_private_out)
    term_shared_out = jnp.einsum(
        "erh,erd->ehd", act_shared, got_gshared, preferred_element_type=jnp.float32
    )
    term_shared_in = jnp.einsum(
        "erd,erh->edh", got_shared, back_grad_shared, preferred_element_type=jnp.float32
    )
    term_private_out = jnp.einsum(
        "erh,erd->ehd", act_private, got_gprivate, preferred_element_type=jnp.float32
    )
    term_private_in = jnp.einsum(
        "erd,erh->edh", got_private, back_grad_private, preferred_element_type=jnp.float32
    )
    summed = (
        lax.psum_scatter(
            term_shared_in.astype(jnp.bfloat16), "batch", scatter_dimension=2, tiled=True
        ).astype(jnp.float32),
        lax.psum_scatter(
            term_shared_out.astype(jnp.bfloat16), "batch", scatter_dimension=1, tiled=True
        ).astype(jnp.float32),
        lax.psum_scatter(
            term_private_in.astype(jnp.bfloat16), "batch", scatter_dimension=2, tiled=True
        ).astype(jnp.float32),
        lax.psum_scatter(
            term_private_out.astype(jnp.bfloat16), "batch", scatter_dimension=1, tiled=True
        ).astype(jnp.float32),
    )
    grad_shared_in = summed[0].astype(jnp.bfloat16)
    grad_shared_out = summed[1].astype(jnp.bfloat16)
    grad_private_in = summed[2].astype(jnp.bfloat16)
    grad_private_out = summed[3].astype(jnp.bfloat16)
    return (
        mixed.astype(jnp.bfloat16),
        grad_shared_in,
        grad_shared_out,
        grad_private_in,
        grad_private_out,
        grad_gate,
    )


def solution(mesh):
    return jax.shard_map(
        body,
        mesh=mesh,
        in_specs=(
            P(("batch", "expert"), None),
            P(("batch", "expert"), None),
            P(("batch", "expert")),
            P(("batch", "expert"), None),
            P(("batch", "expert"), None),
            P(),
            P("expert", None, "batch"),
            P("expert", "batch", None),
            P("expert", None, "batch"),
            P("expert", "batch", None),
        ),
        out_specs=(
            P(("batch", "expert"), None),
            P("expert", None, "batch"),
            P("expert", "batch", None),
            P("expert", None, "batch"),
            P("expert", "batch", None),
            P(("batch", "expert"), None, None),
        ),
        check_vma=False,
    )
```

profile of v0, /device:TPU:1, one launch (start us, length us, event | category | flops | bytes accessed | tf_op | source)
XLA Modules:
  0.0 1748.5 jit_solution(1115050402414843876)
XLA Ops:
  12.3 13.0 all-to-all-start.2
  26.6 16.0 all-to-all-done.2
  42.7 6.3 all-to-all-start
  49.1 17.2 all-to-all-done
  66.4 4.9 fusion.4
  71.4 46.2 %all-gather.11.cloned.1.call-done = bf16[1,2048,1024]{2,1,0:T(8,128)(2,1)} async-done(((bf16[1,512,1024]{2,1,0:T(8,128)(2,1)}), bf16[1,2048,1024]{2,1,0:T(8,128)(2,1)}) %all-gather.11.cloned.1.call-update) | async-done | bytes 4194320 | tf_op jit(solution)/shard_map/all_gather | solution.py:103
  117.6 4.1 fusion.30
  123.0 3.7 reduce
  126.7 1.1 reshape.266
  127.8 10.7 all-to-all-start.3
  138.5 32.1 %all-gather.5.cloned.1.call-done = bf16[1,1024,2048]{2,1,0:T(8,128)(2,1)} async-done(((bf16[1,1024,512]{2,1,0:T(8,128)(2,1)}), bf16[1,1024,2048]{2,1,0:T(8,128)(2,1)}) %all-gather.5.cloned.1.call-update) | async-done | bytes 4194320 | tf_op jit(solution)/shard_map/all_gather | solution.py:100
  170.6 4.8 fusion.10
  175.4 48.1 %all-gather.7.cloned.1.call-done = bf16[1,2048,1024]{2,1,0:T(8,128)(2,1)} async-done(((bf16[1,512,1024]{2,1,0:T(8,128)(2,1)}), bf16[1,2048,1024]{2,1,0:T(8,128)(2,1)}) %all-gather.7.cloned.1.call-update) | async-done | bytes 4194320 | tf_op jit(solution)/shard_map/all_gather | solution.py:101
  223.5 4.1 fusion.33
  228.4 3.7 reduce.1
  232.1 1.1 reshape.268
  233.3 10.7 all-to-all-start.1
  246.6 14.7 all-to-all-done.1
  262.2 1.2 fusion.40
  263.5 1.1 fusion.92
  264.6 3.5 copy.46
  269.8 24.2 %all_to_all.24 = bf16[64,4,1024]{2,1,0:T(4,128)(2,1)S(1)} all-to-all(bf16[64,4,1024]{2,1,0:T(4,128)(2,1)S(1)} %reshape.261), channel_id=1, replica_groups=mesh['batch'=4,'expert'=64] {'expert'}, dimensions={0} | all-to-all | bytes 1048576 | tf_op jit(solution)/shard_map/all_to_all | solution.py:135
  294.1 7.4 convert_bitcast_fusion.3
  301.6 4.9 convert_bitcast_fusion.2
  307.4 23.3 %all_to_all.25 = bf16[64,4,1024]{2,1,0:T(4,128)(2,1)S(1)} all-to-all(bf16[64,4,1024]{2,1,0:T(4,128)(2,1)S(1)} %reshape.263), channel_id=1, replica_groups=mesh['batch'=4,'expert'=64] {'expert'}, dimensions={0} | all-to-all | bytes 1048576 | tf_op jit(solution)/shard_map/all_to_all | solution.py:136
  330.9 7.4 convert_bitcast_fusion.1
  338.4 4.9 convert_bitcast_fusion
  345.4 1189.0 %reduce-scatter.14.cloned.1.call-done = f32[4,8,72]{2,1,0:T(8,128)} async-done(((f32[1024,8,72]{2,1,0:T(8,128)}), f32[4,8,72]{2,1,0:T(8,128)}) %reduce-scatter.14.cloned.1.call-update) | async-done | bytes 9232 | tf_op jit(solution)/shard_map/reduce_scatter | solution.py:133
  1534.4 50.5 %reduce-scatter.6.cloned.1.call-done = bf16[1,1024,512]{2,1,0:T(8,128)(2,1)} async-done(((bf16[1,1024,2048]{2,1,0:T(8,128)(2,1)}), bf16[1,1024,512]{2,1,0:T(8,128)(2,1)}) %reduce-scatter.6.cloned.1.call-update) | async-done | bytes 1048592 | tf_op jit(solution)/shard_map/reduce_scatter | solution.py:153
  1584.9 52.3 %reduce-scatter.8.cloned.1.call-done = bf16[1,512,1024]{2,1,0:T(8,128)(2,1)} async-done(((bf16[1,2048,1024]{2,1,0:T(8,128)(2,1)}), bf16[1,512,1024]{2,1,0:T(8,128)(2,1)}) %reduce-scatter.8.cloned.1.call-update) | async-done | bytes 1048592 | tf_op jit(solution)/shard_map/reduce_scatter | solution.py:156
  1637.2 52.4 %reduce-scatter.10.cloned.1.call-done = bf16[1,1024,512]{2,1,0:T(8,128)(2,1)} async-done(((bf16[1,1024,2048]{2,1,0:T(8,128)(2,1)}), bf16[1,1024,512]{2,1,0:T(8,128)(2,1)}) %reduce-scatter.10.cloned.1.call-update) | async-done | bytes 1048592 | tf_op jit(solution)/shard_map/reduce_scatter | solution.py:159
  1689.6 52.3 %reduce-scatter.12.cloned.1.call-done = bf16[1,512,1024]{2,1,0:T(8,128)(2,1)} async-done(((bf16[1,2048,1024]{2,1,0:T(8,128)(2,1)}), bf16[1,512,1024]{2,1,0:T(8,128)(2,1)}) %reduce-scatter.12.cloned.1.call-update) | async-done | bytes 1048592 | tf_op jit(solution)/shard_map/reduce_scatter | solution.py:162
  (93 shorter events, 17.3 us)
Async XLA Ops:
  7.2 237.5 %copy-start = (bf16[1024,8,72]{0,2,1:T(8,128)(2,1)S(1)}, bf16[1024,8,72]{0,2,1:T(8,128)(2,1)}, u32[]{:S(2)}) copy-start(bf16[1024,8,72]{0,2,1:T(8,128)(2,1)} %param.15) | copy-start | bytes 3538948
  7.2 2.8 copy-start.13
  7.2 3.0 copy-start.15
  7.2 3.1 copy-start.14
  7.2 3.8 copy-start.4
  7.2 59.2 %all-gather.9.cloned.1.call-start = ((), (), s32[]{:S(2)}) async-start(), calls=%async_computation.13 | async-start | bytes 5242880 | tf_op jit(solution)/shard_map/all_gather | solution.py:102
  8.0 109.6 %all-gather.11.cloned.1.call-start = ((), (), s32[]{:S(2)}) async-start(), calls=%async_computation.14 | async-start | bytes 5242880 | tf_op jit(solution)/shard_map/all_gather | solution.py:103
  8.7 161.9 %all-gather.5.cloned.1.call-start = ((), (), s32[]{:S(2)}) async-start(), calls=%async_computation.11 | async-start | bytes 5242880 | tf_op jit(solution)/shard_map/all_gather | solution.py:100
  9.4 214.1 %all-gather.7.cloned.1.call-start = ((), (), s32[]{:S(2)}) async-start(), calls=%async_computation.12 | async-start | bytes 5242880 | tf_op jit(solution)/shard_map/all_gather | solution.py:101
  12.3 30.3 %all-to-all-start.2 = ((bf16[64,4,1024]{2,1,0:T(4,128)(2,1)}), bf16[64,4,1024]{2,1,0:T(4,128)(2,1)S(1)}, u32[]{:S(2)}, u32[]{:S(2)}) async-start(bf16[64,4,1024]{2,1,0:T(4,128)(2,1)} %reshape.256), calls=%async_computation.2 | async-start | bytes 1048576 | tf_op jit(solution)/shard_map/all_to_all | solution.py:97
  42.7 23.6 %all-to-all-start = ((bf16[64,4,1024]{2,1,0:T(4,128)(2,1)}), bf16[64,4,1024]{2,1,0:T(4,128)(2,1)S(1)}, u32[]{:S(2)}, u32[]{:S(2)}) async-start(bf16[64,4,1024]{2,1,0:T(4,128)(2,1)} %reshape.251), calls=%async_computation | async-start | bytes 1048576 | tf_op jit(solution)/shard_map/all_to_all | solution.py:96
  49.1 22.3 %copy-start.9 = (bf16[256,1024]{1,0:T(8,128)(2,1)}, bf16[256,1024]{1,0:T(8,128)(2,1)S(1)}, u32[]{:S(2)}) copy-start(bf16[256,1024]{1,0:T(8,128)(2,1)S(1)} %reshape.257) | copy-start | bytes 1572868
  66.4 104.2 %copy-start.11 = (bf16[256,1024]{1,0:T(8,128)(2,1)}, bf16[256,1024]{1,0:T(8,128)(2,1)S(1)}, u32[]{:S(2)}) copy-start(bf16[256,1024]{1,0:T(8,128)(2,1)S(1)} %reshape.252) | copy-start | bytes 1572868
  127.8 105.4 %all-to-all-start.3 = ((bf16[64,2,2048]{2,1,0:T(2,128)(2,1)}), bf16[64,2,2048]{2,1,0:T(2,128)(2,1)S(1)}, u32[]{:S(2)}, u32[]{:S(2)}) async-start(bf16[64,2,2048]{2,1,0:T(2,128)(2,1)} %reshape.266), calls=%async_computation.3 | async-start | bytes 1048576 | tf_op jit(solution)/shard_map/all_to_all | solution.py:115
  233.3 28.0 %all-to-all-start.1 = ((bf16[64,2,2048]{2,1,0:T(2,128)(2,1)}), bf16[64,2,2048]{2,1,0:T(2,128)(2,1)S(1)}, u32[]{:S(2)}, u32[]{:S(2)}) async-start(bf16[64,2,2048]{2,1,0:T(2,128)(2,1)} %reshape.268), calls=%async_computation.1 | async-start | bytes 1048576 | tf_op jit(solution)/shard_map/all_to_all | solution.py:112
  243.9 1290.4 %reduce-scatter.14.cloned.1.call-start = ((), (), s32[]{:S(2)}) async-start(), calls=%async_computation.19 | async-start | bytes 4210688 | tf_op jit(solution)/shard_map/reduce_scatter | solution.py:133
  246.2 15.9 copy-start.6
  261.8 1.7 copy-start.5
  262.1 2.5 copy-start.2
  268.1 0.9 copy-start.7
  268.1 26.0 %copy-start.12 = (bf16[256,1024]{1,0:T(8,128)(2,1)S(1)}, bf16[256,1024]{1,0:T(8,128)(2,1)}, u32[]{:S(2)}) copy-start(bf16[256,1024]{1,0:T(8,128)(2,1)} %copy-done.11) | copy-start | bytes 1572868
  268.1 1316.8 %reduce-scatter.6.cloned.1.call-start = ((), (), s32[]{:S(2)}) async-start(), calls=%async_computation.15 | async-start | bytes 5242880 | tf_op jit(solution)/shard_map/reduce_scatter | solution.py:153
  301.6 1335.6 %reduce-scatter.8.cloned.1.call-start = ((), (), s32[]{:S(2)}) async-start(), calls=%async_computation.16 | async-start | bytes 5242880 | tf_op jit(solution)/shard_map/reduce_scatter | solution.py:156
  306.6 24.3 %copy-start.10 = (bf16[256,1024]{1,0:T(8,128)(2,1)S(1)}, bf16[256,1024]{1,0:T(8,128)(2,1)}, u32[]{:S(2)}) copy-start(bf16[256,1024]{1,0:T(8,128)(2,1)} %copy-done.9) | copy-start | bytes 1572868
  306.6 1383.0 %reduce-scatter.10.cloned.1.call-start = ((), (), s32[]{:S(2)}) async-start(), calls=%async_computation.17 | async-start | bytes 5242880 | tf_op jit(solution)/shard_map/reduce_scatter | solution.py:159
  338.3 1403.6 %reduce-scatter.12.cloned.1.call-start = ((), (), s32[]{:S(2)}) async-start(), calls=%async_computation.18 | async-start | bytes 5242880 | tf_op jit(solution)/shard_map/reduce_scatter | solution.py:162
  343.3 1.0 copy-start.3
  343.3 1.2 copy-start.8
  343.3 1398.6 %copy-start.1 = (bf16[1024,8,72]{0,2,1:T(8,128)(2,1)S(1)}, bf16[1024,8,72]{0,2,1:T(8,128)(2,1)}, u32[]{:S(2)}) copy-start(bf16[1024,8,72]{0,2,1:T(8,128)(2,1)} %param.15) | copy-start | bytes 3538948
Sparse Core Ops, SparseCore 0:
  9.9 54.5 all-gather.8
  66.3 51.2 all-gather.10
  119.4 51.1 all-gather.4
  172.2 51.2 all-gather.6
  268.2 1266.0 reduce-scatter.13
  1537.5 47.3 reduce-scatter.5
  1588.0 49.1 reduce-scatter.7
  1640.5 49.1 reduce-scatter.9
  1692.8 49.1 reduce-scatter.11
where the time goes:
time: 1750 us
  waiting for transfers between devices  1570 us (90%)
  matrix products  48.2 us (3%)
  blocking collectives  47.5 us (3%)
  starting transfers between devices  41.2 us (2%)
    reduce_scatter x1, waiting for transfers between devices, body(): lax.psum_scatter(gate_term, ('batch', 'expert'), scatter_dimension=0, til...  1190 us
    reduce_scatter x1, waiting for transfers between devices, body(): lax.psum_scatter(term_private_in.astype(jnp.bfloat16), 'batch', scatter_d...  52.4 us
    reduce_scatter x1, waiting for transfers between devices, body(): lax.psum_scatter(term_private_out.astype(jnp.bfloat16), 'batch', scatter_...  52.3 us
    reduce_scatter x1, waiting for transfers between devices, body(): lax.psum_scatter(term_shared_out.astype(jnp.bfloat16), 'batch', scatter_d...  52.3 us
    reduce_scatter x1, waiting for transfers between devices, body(): lax.psum_scatter(term_shared_in.astype(jnp.bfloat16), 'batch', scatter_di...  50.5 us
    all_gather x1, waiting for transfers between devices, body(): lax.all_gather(shared_out, 'batch', axis=1, tiled=True)  48.1 us
    all_gather x1, waiting for transfers between devices, body(): lax.all_gather(private_out, 'batch', axis=1, tiled=True)  46.2 us
  transfers between devices with their start and end apart: 13, of which 11 were waited for; matrix products, arithmetic and copies ran while one was open for 4% of the time, Pallas kernels for 0%

commit v1 on v0

--- a/solution.py
+++ b/solution.py
@@ -9,6 +9,22 @@
 PRIVATE = 64
 GATES = 72
 CAP = 4
+
+
+def gather_around(x, axis, dim):
+    ways, here, step = (lax.axis_size(axis), lax.axis_index(axis), x.shape[dim])
+    shape = [n * ways if d == dim else n for d, n in enumerate(x.shape)]
+    full = lax.dynamic_update_slice_in_dim(jnp.zeros(shape, x.dtype), x, here * step, axis=dim)
+    going_up = going_down = x
+    for far in range(1, ways // 2 + 1):
+        going_up = lax.ppermute(going_up, axis, [(d, (d + 1) % ways) for d in range(ways)])
+        full = lax.dynamic_update_slice_in_dim(full, going_up, (here - far) % ways * step, axis=dim)
+        if 2 * far < ways:
+            going_down = lax.ppermute(going_down, axis, [(d, (d - 1) % ways) for d in range(ways)])
+            full = lax.dynamic_update_slice_in_dim(
+                full, going_down, (here + far) % ways * step, axis=dim
+            )
+    return full
 
 
 def silu_slope(values):
@@ -98,7 +114,7 @@
     )
     full_shared_in, full_shared_out, full_private_in, full_private_out = (
         lax.all_gather(shared_in, "batch", axis=2, tiled=True),
-        lax.all_gather(shared_out, "batch", axis=1, tiled=True),
+        gather_around(shared_out, "batch", 1),
         lax.all_gather(private_in, "batch", axis=2, tiled=True),
         lax.all_gather(private_out, "batch", axis=1, tiled=True),
     )

time: 1750 us -> 1730 us (0.989)
  waiting for transfers between devices: 1570 us -> 1540 us
    all_gather x1 -> x0, waiting for transfers between devices: 48.1 us -> none  [body(): lax.all_gather(shared_out, 'batch', axis=1, tiled=True)]
    ppermute x0 -> x3, waiting for transfers between devices: none -> 43.2 us  [the longest x2 36 us: gather_around(): lax.ppermute(going_up, axis, [(d, (d + 1) % ways) for d in range(ways)])]
  transfers between devices with their start and end apart: 13 -> 15, of which waited for: 11 -> 12; matrix products, arithmetic and copies ran while one was open for 4% -> 4% of each run, Pallas kernels for 0% -> 0%
where the time goes in v1:
time: 1730 us
  waiting for transfers between devices  1540 us (89%)
  starting transfers between devices  47.7 us (3%)
  blocking collectives  47.3 us (3%)
  matrix products  47.2 us (3%)
  local copies, waits for them, and re-layouts  25.8 us (1%)
    reduce_scatter x1, waiting for transfers between devices, body(): lax.psum_scatter(gate_term, ('batch', 'expert'), scatter_dimension=0, til...  1190 us
    reduce_scatter x1, waiting for transfers between devices, body(): lax.psum_scatter(term_private_in.astype(jnp.bfloat16), 'batch', scatter_d...  52.4 us
    reduce_scatter x1, waiting for transfers between devices, body(): lax.psum_scatter(term_private_out.astype(jnp.bfloat16), 'batch', scatter_...  52.3 us
    reduce_scatter x1, waiting for transfers between devices, body(): lax.psum_scatter(term_shared_out.astype(jnp.bfloat16), 'batch', scatter_d...  52.1 us
    reduce_scatter x1, waiting for transfers between devices, body(): lax.psum_scatter(term_shared_in.astype(jnp.bfloat16), 'batch', scatter_di...  50.5 us
    ppermute x2, waiting for transfers between devices, gather_around(): lax.ppermute(going_up, axis, [(d, (d + 1) % ways) for d in range(ways)])  36 us
  transfers between devices with their start and end apart: 15, of which 12 were waited for; matrix products, arithmetic and copies ran while one was open for 4% of the time, Pallas kernels for 0%

profile of v1, /device:TPU:1, one launch (start us, length us, event | category | flops | bytes accessed | tf_op | source)
XLA Modules:
  0.0 1729.2 jit_solution(17913941408150616854)
XLA Ops:
  11.8 13.0 all-to-all-start.2
  27.4 14.7 all-to-all-done.2
  42.1 6.3 all-to-all-start
  48.4 2.8 collective-permute-start.1
  51.2 19.1 %collective-permute-done = bf16[1,512,1024]{2,1,0:T(8,128)(2,1)} collective-permute-done((bf16[1,512,1024]{2,1,0:T(8,128)(2,1)S(1)}, bf16[1,512,1024]{2,1,0:T(8,128)(2,1)}, u32[]{:S(2)}, u32[]{:S(2)}) %collective-permute-start) | collective-permute-done | bytes 1048608 | tf_op jit(solution)/shard_map/ppermute | solution.py:20
  72.4 2.5 broadcast.97
  80.2 7.2 collective-permute-done.1
  89.6 16.9 collective-permute-done.2
  106.5 2.3 bitcast_dynamic-update-slice_fusion
  108.8 5.0 fusion.4
  113.9 33.2 %all-gather.8.cloned.1.call-done = bf16[1,2048,1024]{2,1,0:T(8,128)(2,1)} async-done(((bf16[1,512,1024]{2,1,0:T(8,128)(2,1)}), bf16[1,2048,1024]{2,1,0:T(8,128)(2,1)}) %all-gather.8.cloned.1.call-update) | async-done | bytes 4194320 | tf_op jit(solution)/shard_map/all_gather | solution.py:119
  147.1 4.1 fusion.19
  152.5 3.7 reduce
  157.4 10.9 all-to-all-start.3
  168.3 31.8 %all-gather.4.cloned.1.call-done = bf16[1,1024,2048]{2,1,0:T(8,128)(2,1)} async-done(((bf16[1,1024,512]{2,1,0:T(8,128)(2,1)}), bf16[1,1024,2048]{2,1,0:T(8,128)(2,1)}) %all-gather.4.cloned.1.call-update) | async-done | bytes 4194320 | tf_op jit(solution)/shard_map/all_gather | solution.py:116
  200.1 3.4 fusion.6
  203.5 4.3 fusion.18
  208.6 3.7 reduce.1
  213.5 10.7 all-to-all-start.1
  226.8 14.7 all-to-all-done.1
  244.8 3.5 copy.46
  250.0 24.2 %all_to_all.24 = bf16[64,4,1024]{2,1,0:T(4,128)(2,1)S(1)} all-to-all(bf16[64,4,1024]{2,1,0:T(4,128)(2,1)S(1)} %reshape.278), channel_id=1, replica_groups=mesh['batch'=4,'expert'=64] {'expert'}, dimensions={0} | all-to-all | bytes 1048576 | tf_op jit(solution)/shard_map/all_to_all | solution.py:151
  274.3 7.4 convert_bitcast_fusion.3
  281.8 4.9 convert_bitcast_fusion.2
  287.6 23.2 %all_to_all.25 = bf16[64,4,1024]{2,1,0:T(4,128)(2,1)S(1)} all-to-all(bf16[64,4,1024]{2,1,0:T(4,128)(2,1)S(1)} %reshape.280), channel_id=1, replica_groups=mesh['batch'=4,'expert'=64] {'expert'}, dimensions={0} | all-to-all | bytes 1048576 | tf_op jit(solution)/shard_map/all_to_all | solution.py:152
  311.0 7.4 convert_bitcast_fusion.1
  318.4 4.9 convert_bitcast_fusion
  325.5 1189.3 %reduce-scatter.14.cloned.1.call-done = f32[4,8,72]{2,1,0:T(8,128)} async-done(((f32[1024,8,72]{2,1,0:T(8,128)}), f32[4,8,72]{2,1,0:T(8,128)}) %reduce-scatter.14.cloned.1.call-update) | async-done | bytes 9232 | tf_op jit(solution)/shard_map/reduce_scatter | solution.py:149
  1514.7 50.5 %reduce-scatter.6.cloned.1.call-done = bf16[1,1024,512]{2,1,0:T(8,128)(2,1)} async-done(((bf16[1,1024,2048]{2,1,0:T(8,128)(2,1)}), bf16[1,1024,512]{2,1,0:T(8,128)(2,1)}) %reduce-scatter.6.cloned.1.call-update) | async-done | bytes 1048592 | tf_op jit(solution)/shard_map/reduce_scatter | solution.py:169
  1565.3 52.1 %reduce-scatter.8.cloned.1.call-done = bf16[1,512,1024]{2,1,0:T(8,128)(2,1)} async-done(((bf16[1,2048,1024]{2,1,0:T(8,128)(2,1)}), bf16[1,512,1024]{2,1,0:T(8,128)(2,1)}) %reduce-scatter.8.cloned.1.call-update) | async-done | bytes 1048592 | tf_op jit(solution)/shard_map/reduce_scatter | solution.py:172
  1617.4 52.4 %reduce-scatter.10.cloned.1.call-done = bf16[1,1024,512]{2,1,0:T(8,128)(2,1)} async-done(((bf16[1,1024,2048]{2,1,0:T(8,128)(2,1)}), bf16[1,1024,512]{2,1,0:T(8,128)(2,1)}) %reduce-scatter.10.cloned.1.call-update) | async-done | bytes 1048592 | tf_op jit(solution)/shard_map/reduce_scatter | solution.py:175
  1669.9 52.3 %reduce-scatter.12.cloned.1.call-done = bf16[1,512,1024]{2,1,0:T(8,128)(2,1)} async-done(((bf16[1,2048,1024]{2,1,0:T(8,128)(2,1)}), bf16[1,512,1024]{2,1,0:T(8,128)(2,1)}) %reduce-scatter.12.cloned.1.call-update) | async-done | bytes 1048592 | tf_op jit(solution)/shard_map/reduce_scatter | solution.py:178
  (105 shorter events, 31.9 us)
Async XLA Ops:
  7.2 217.8 %copy-start = (bf16[1024,8,72]{0,2,1:T(8,128)(2,1)S(1)}, bf16[1024,8,72]{0,2,1:T(8,128)(2,1)}, u32[]{:S(2)}) copy-start(bf16[1024,8,72]{0,2,1:T(8,128)(2,1)} %param.15) | copy-start | bytes 3538948
  7.2 2.3 copy-start.14
  7.2 2.5 copy-start.16
  7.2 2.5 copy-start.15
  7.2 3.3 copy-start.4
  7.2 101.6 %all-gather.6.cloned.1.call-start = ((), (), s32[]{:S(2)}) async-start(), calls=%async_computation.12 | async-start | bytes 5242880 | tf_op jit(solution)/shard_map/all_gather | solution.py:118
  8.0 139.1 %all-gather.8.cloned.1.call-start = ((), (), s32[]{:S(2)}) async-start(), calls=%async_computation.13 | async-start | bytes 5242880 | tf_op jit(solution)/shard_map/all_gather | solution.py:119
  8.7 16.1 copy-start.9
  8.7 191.4 %all-gather.4.cloned.1.call-start = ((), (), s32[]{:S(2)}) async-start(), calls=%async_computation.11 | async-start | bytes 5242880 | tf_op jit(solution)/shard_map/all_gather | solution.py:116
  11.8 30.3 %all-to-all-start.2 = ((bf16[64,4,1024]{2,1,0:T(4,128)(2,1)}), bf16[64,4,1024]{2,1,0:T(4,128)(2,1)S(1)}, u32[]{:S(2)}, u32[]{:S(2)}) async-start(bf16[64,4,1024]{2,1,0:T(4,128)(2,1)} %reshape.273), calls=%async_computation.2 | async-start | bytes 1048576 | tf_op jit(solution)/shard_map/all_to_all | solution.py:113
  24.8 45.6 %collective-permute-start = (bf16[1,512,1024]{2,1,0:T(8,128)(2,1)S(1)}, bf16[1,512,1024]{2,1,0:T(8,128)(2,1)}, u32[]{:S(2)}, u32[]{:S(2)}) collective-permute-start(bf16[1,512,1024]{2,1,0:T(8,128)(2,1)S(1)} %copy-done.9), channel_id=1, source_target_pairs={{0,64},{64,128},{128,192},{192,0},{1,65},{65,129},{129,193},{193,1... | collective-permute-start | bytes 3145736 | tf_op jit(solution)/shard_map/ppermute | solution.py:20
  42.1 34.8 %all-to-all-start = ((bf16[64,4,1024]{2,1,0:T(4,128)(2,1)}), bf16[64,4,1024]{2,1,0:T(4,128)(2,1)S(1)}, u32[]{:S(2)}, u32[]{:S(2)}) async-start(bf16[64,4,1024]{2,1,0:T(4,128)(2,1)} %reshape.265), calls=%async_computation | async-start | bytes 1048576 | tf_op jit(solution)/shard_map/all_to_all | solution.py:112
  48.4 38.9 %collective-permute-start.1 = (bf16[1,512,1024]{2,1,0:T(8,128)(2,1)S(1)}, bf16[1,512,1024]{2,1,0:T(8,128)(2,1)}, u32[]{:S(2)}, u32[]{:S(2)}) collective-permute-start(bf16[1,512,1024]{2,1,0:T(8,128)(2,1)S(1)} %copy-done.9), channel_id=1, source_target_pairs={{0,192},{64,0},{128,64},{192,128},{1,193},{65,1},{129,65},{193,129... | collective-permute-start | bytes 3145736 | tf_op jit(solution)/shard_map/ppermute | solution.py:23
  70.3 36.1 %collective-permute-start.2 = (bf16[1,512,1024]{2,1,0:T(8,128)(2,1)}, bf16[1,512,1024]{2,1,0:T(8,128)(2,1)}, u32[]{:S(2)}, u32[]{:S(2)}) collective-permute-start(bf16[1,512,1024]{2,1,0:T(8,128)(2,1)} %collective-permute-done), channel_id=1, source_target_pairs={{0,64},{64,128},{128,192},{192,0},{1,65},{65,129},{129,193},{193,1... | collective-permute-start | bytes 3145736 | tf_op jit(solution)/shard_map/ppermute | solution.py:20
  80.1 28.7 %copy-start.10 = (bf16[256,1024]{1,0:T(8,128)(2,1)S(1)}, bf16[256,1024]{1,0:T(8,128)(2,1)}, u32[]{:S(2)}) copy-start(bf16[256,1024]{1,0:T(8,128)(2,1)} %reshape.274) | copy-start | bytes 1572868
  152.0 48.1 %copy-start.12 = (bf16[256,1024]{1,0:T(8,128)(2,1)S(1)}, bf16[256,1024]{1,0:T(8,128)(2,1)}, u32[]{:S(2)}) copy-start(bf16[256,1024]{1,0:T(8,128)(2,1)} %reshape.266) | copy-start | bytes 1572868
  157.4 56.1 %all-to-all-start.3 = ((bf16[64,2,2048]{2,1,0:T(2,128)(2,1)}), bf16[64,2,2048]{2,1,0:T(2,128)(2,1)S(1)}, u32[]{:S(2)}, u32[]{:S(2)}) async-start(bf16[64,2,2048]{2,1,0:T(2,128)(2,1)} %reshape.283), calls=%async_computation.3 | async-start | bytes 1048576 | tf_op jit(solution)/shard_map/all_to_all | solution.py:131
  203.5 4.3 copy-start.17
  213.5 28.0 %all-to-all-start.1 = ((bf16[64,2,2048]{2,1,0:T(2,128)(2,1)}), bf16[64,2,2048]{2,1,0:T(2,128)(2,1)S(1)}, u32[]{:S(2)}, u32[]{:S(2)}) async-start(bf16[64,2,2048]{2,1,0:T(2,128)(2,1)} %reshape.285), calls=%async_computation.1 | async-start | bytes 1048576 | tf_op jit(solution)/shard_map/all_to_all | solution.py:128
  224.2 1290.6 %reduce-scatter.14.cloned.1.call-start = ((), (), s32[]{:S(2)}) async-start(), calls=%async_computation.18 | async-start | bytes 4210688 | tf_op jit(solution)/shard_map/reduce_scatter | solution.py:149
  226.5 15.9 copy-start.6
  242.0 1.7 copy-start.5
  242.4 2.5 copy-start.2
  248.4 26.0 %copy-start.13 = (bf16[256,1024]{1,0:T(8,128)(2,1)S(1)}, bf16[256,1024]{1,0:T(8,128)(2,1)}, u32[]{:S(2)}) copy-start(bf16[256,1024]{1,0:T(8,128)(2,1)} %reshape.266) | copy-start | bytes 1572868
  248.4 1316.9 %reduce-scatter.6.cloned.1.call-start = ((), (), s32[]{:S(2)}) async-start(), calls=%async_computation.14 | async-start | bytes 5242880 | tf_op jit(solution)/shard_map/reduce_scatter | solution.py:169
  281.8 1335.6 %reduce-scatter.8.cloned.1.call-start = ((), (), s32[]{:S(2)}) async-start(), calls=%async_computation.15 | async-start | bytes 5242880 | tf_op jit(solution)/shard_map/reduce_scatter | solution.py:172
  286.8 24.1 %copy-start.11 = (bf16[256,1024]{1,0:T(8,128)(2,1)S(1)}, bf16[256,1024]{1,0:T(8,128)(2,1)}, u32[]{:S(2)}) copy-start(bf16[256,1024]{1,0:T(8,128)(2,1)} %reshape.274) | copy-start | bytes 1572868
  286.8 1383.0 %reduce-scatter.10.cloned.1.call-start = ((), (), s32[]{:S(2)}) async-start(), calls=%async_computation.16 | async-start | bytes 5242880 | tf_op jit(solution)/shard_map/reduce_scatter | solution.py:175
  318.4 1403.8 %reduce-scatter.12.cloned.1.call-start = ((), (), s32[]{:S(2)}) async-start(), calls=%async_computation.17 | async-start | bytes 5242880 | tf_op jit(solution)/shard_map/reduce_scatter | solution.py:178
  323.4 1.0 copy-start.3
  323.4 1.2 copy-start.8
  323.4 1398.8 %copy-start.1 = (bf16[1024,8,72]{0,2,1:T(8,128)(2,1)S(1)}, bf16[1024,8,72]{0,2,1:T(8,128)(2,1)}, u32[]{:S(2)}) copy-start(bf16[1024,8,72]{0,2,1:T(8,128)(2,1)} %param.15) | copy-start | bytes 3538948
  (1 other events, 0.9 us)
Sparse Core Ops, SparseCore 0:
  9.9 84.4 all-gather.5
  96.2 50.8 all-gather.7
  148.9 51.1 all-gather.3
  248.5 1266.2 reduce-scatter.13
  1517.9 47.3 reduce-scatter.5
  1568.2 49.1 reduce-scatter.7
  1620.7 49.1 reduce-scatter.9
  1673.0 49.1 reduce-scatter.11
